TPU v7x, 256 devices: a whole 4x4x8 slice. The times are simulated.
256 devices in a mesh: rep: 16 (over z_hi, x), fsdp: 16 (over z_lo, y, core).
Axes of the slice: x: 4, y: 4, z: 8 (z_hi: 4, z_lo: 2; z = z_hi * 2 + z_lo), core: 2. Of those that a mesh axis runs over, the one named last changes fastest.
Arguments:
- layer_input: bfloat16 [16, 2, 4096, 5120], P('rep', None, 'fsdp'), may hold values from -6 to 6
- cotangent: bfloat16 [16, 2, 4096, 512], P('rep', None, 'fsdp'), may hold values from -6 to 6
- key_weight: bfloat16 [16, 5120, 512], P('rep', 'fsdp'), may hold values from -6 to 6
- key_gain: float32 [512], replicated, may hold values from 0.1 to 1.9
- fragment: bfloat16 [16, 5120, 512], P('rep', 'fsdp'), may hold values from -6 to 6
- outer_params: float32 [5120, 512], P('fsdp', 'rep'), may hold values from -6 to 6
- outer_momentum: float32 [5120, 512], P('fsdp', 'rep'), may hold values from -3 to 3
- plan: int32 [1], replicated, may hold values from 0 to 63
Outputs:
- new_key_weight: bfloat16 [16, 5120, 512], P('rep', 'fsdp')
- new_fragment: bfloat16 [16, 5120, 512], P('rep', 'fsdp')
- new_outer: float32 [5120, 512], P('fsdp', 'rep')
- new_momentum: float32 [5120, 512], P('fsdp', 'rep')
All inputs are finite; a program needn't handle non-finite values.
Results may differ from a plain program's by a relative error of at most 0.014.
Values may be sent and summed in bfloat16 or wider, within the bound.
A program may use at most 128 MiB of HBM per device.

v0:
```python
import math

import jax
import jax.numpy as jnp
from jax import lax
from jax.sharding import PartitionSpec as P

D = 5120
HD = 128
STEPS = 2
ROUNDS = 64


MOMENTUM_DECAY = 0.9
OUTER_RATE = 0.7
LOCAL_SHARE = 0.25


def key_backward(key_values, cot_rows, key_gain):
    head_count = key_values.shape[1] // HD
    heads_view = key_values.reshape(key_values.shape[0], head_count, HD)
    root_mean = jnp.sqrt(jnp.mean(heads_view * heads_view, axis=-1, keepdims=True) + 1e-06)
    normalized = heads_view / root_mean
    pulled = cot_rows.astype(jnp.float32).reshape(heads_view.shape) * key_gain.reshape(
        head_count, HD
    )
    key_slope = (
        pulled - normalized * jnp.mean(pulled * normalized, axis=-1, keepdims=True)
    ) / root_mean
    return key_slope.reshape(key_values.shape).astype(jnp.bfloat16)


def project_keys(inputs, weight_rows):
    return jnp.dot(
        inputs,
        lax.all_gather(weight_rows, "fsdp", axis=0, tiled=True),
        preferred_element_type=jnp.float32,
    )


def grad_rows(inputs, key_slope, key_scale):
    return lax.psum_scatter(
        (
            key_scale
            * lax.dot_general(
                inputs, key_slope, (((0,), (0,)), ((), ())), preferred_element_type=jnp.float32
            )
        ).astype(jnp.bfloat16),
        "fsdp",
        scatter_dimension=0,
        tiled=True,
    ).astype(jnp.float32)


def nesterov(outer_old, moment, group_mean, outer_factor):
    pseudo_grad = outer_old - group_mean
    moment_new = MOMENTUM_DECAY * moment + pseudo_grad
    outer_new = outer_old - outer_factor * (pseudo_grad + MOMENTUM_DECAY * moment_new)
    return (outer_new, moment_new)


def shards(
    layer_input, cotangent, key_weight, key_gain, fragment, outer_params, outer_momentum, plan
):
    inputs_all = layer_input[0]
    cot_steps = cotangent[0]
    weight_rows = key_weight[0]
    tokens_all = inputs_all.shape[1] * lax.axis_size("fsdp")
    key_scale = D ** (-0.5)
    inner_rate = 0.5 * math.sqrt(D / tokens_all)
    for inner_step in range(STEPS):
        key_values = project_keys(inputs_all[inner_step], weight_rows) * key_scale
        key_slope = key_backward(key_values, cot_steps[inner_step], key_gain)
        gradient = grad_rows(inputs_all[inner_step], key_slope, key_scale)
        weight_rows = (weight_rows.astype(jnp.float32) - inner_rate * gradient).astype(jnp.bfloat16)
    frag_rows = fragment[0].astype(jnp.float32)
    group_count = lax.axis_size("rep")
    outer_factor = OUTER_RATE * (
        0.55 + 0.45 * jnp.cos(math.pi * plan[0].astype(jnp.float32) / ROUNDS)
    )
    portion = lax.psum_scatter(
        frag_rows.astype(jnp.bfloat16), "rep", scatter_dimension=1, tiled=True
    ).astype(jnp.float32)
    new_outer, new_moment = nesterov(
        outer_params, outer_momentum, portion / group_count, outer_factor
    )
    outer_full = lax.all_gather(new_outer.astype(jnp.bfloat16), "rep", axis=1, tiled=True).astype(
        new_outer.dtype
    )
    blended = (LOCAL_SHARE * frag_rows + (1.0 - LOCAL_SHARE) * outer_full).astype(jnp.bfloat16)
    return (weight_rows[None], blended[None], new_outer, new_moment)


def solution(mesh):
    placed = (
        P("rep", None, "fsdp", None),
        P("rep", None, "fsdp", None),
        P("rep", "fsdp", None),
        P(),
        P("rep", "fsdp", None),
        P("fsdp", "rep"),
        P("fsdp", "rep"),
        P(),
    )
    return jax.shard_map(
        shards,
        mesh=mesh,
        in_specs=placed,
        out_specs=(
            P("rep", "fsdp", None),
            P("rep", "fsdp", None),
            P("fsdp", "rep"),
            P("fsdp", "rep"),
        ),
        check_vma=False,
    )
```

profile of v0, /device:TPU:1, one launch (start us, length us, event | category | flops | bytes accessed | tf_op | source)
XLA Modules:
  0.0 319.7 jit_solution(16835928184684568395)
XLA Ops:
  8.0 0.7 all-gather.6.cloned.1.call-update
  8.8 1.2 slice_convert_fusion
  9.9 0.2 reshape.106
  10.2 46.8 %all-gather.6.cloned.1.call-done = bf16[1,5120,512]{2,1,0:T(8,128)(2,1)} async-done(((bf16[1,320,512]{2,1,0:T(8,128)(2,1)}), bf16[1,5120,512]{2,1,0:T(8,128)(2,1)}) %all-gather.6.cloned.1.call-update) | async-done | bytes 5242896 | tf_op jit(solution)/shard_map/all_gather | solution.py:36
  57.0 4.8 %fusion.19 = f32[256,512]{1,0:T(8,128)S(1)} fusion(bf16[1,5120,512]{2,1,0:T(8,128)(2,1)} %all-gather.6.cloned.1.call-done, bf16[1,2,256,5120]{3,2,1,0:T(8,128)(2,1)} %param.8), kind=kOutput, calls=%fused_computation.17 | convolution fusion | flops 1342308352 | bytes 8388608 | tf_op jit(solution)/shard_map/dot_general | solution.py:34
  62.0 0.3 multiply_reduce_fusion.1
  62.4 0.6 fusion.31
  63.1 0.3 mul.129
  63.4 0.3 div.70
  63.7 5.8 %fusion = bf16[5120,512]{0,1:T(8,128)(2,1)} fusion(bf16[1,2,256,5120]{3,2,1,0:T(8,128)(2,1)} %param.8, f32[32,8,4,128]{3,2,1,0:T(4,128)S(1)} %bitcast.97, f32[256,512]{1,0:T(8,128)S(1)} %fusion.19, f32[32,8,4,128]{3,2,1,0:T(4,128)S(1)} %bitcast.99, f32[512]{0:T(512)S(1)} %copy-done.5, bf16[1,2,256,512]{3,2,1,0:T(8,128)(2,1)S(1)} %copy-done.2), kind=kOutput, calls=%fused_computation.2 | convolution fusion | flops 1348337664 | bytes 9701376 | tf_op jit(solution)/shard_map/dot_general | solution.py:45
  69.5 8.0 %copy.42 = bf16[5120,512]{1,0:T(8,128)(2,1)} copy(bf16[5120,512]{0,1:T(8,128)(2,1)} %fusion) | data formatting | bytes 10485760
  77.6 0.9 copy-done
  78.4 0.2 copy.35
  78.7 66.2 %reduce-scatter.10.cloned.1.call-done = bf16[320,512]{1,0:T(8,128)(2,1)} async-done(((bf16[5120,512]{1,0:T(8,128)(2,1)}), bf16[320,512]{1,0:T(8,128)(2,1)}) %reduce-scatter.10.cloned.1.call-update) | async-done | bytes 327696
  144.9 1.2 copy.43
  146.2 0.9 copy.36
  147.2 1.0 copy.46
  148.4 43.3 %all-gather.4.cloned.1.call-done = bf16[5120,512]{1,0:T(8,128)(2,1)} async-done(((bf16[320,512]{1,0:T(8,128)(2,1)}), bf16[5120,512]{1,0:T(8,128)(2,1)}) %all-gather.4.cloned.1.call-update) | async-done | bytes 5242896 | tf_op jit(solution)/shard_map/all_gather | solution.py:36
  191.7 4.8 %fusion.16 = f32[256,512]{1,0:T(8,128)S(1)} fusion(bf16[5120,512]{1,0:T(8,128)(2,1)} %all-gather.4.cloned.1.call-done, bf16[1,2,256,5120]{3,2,1,0:T(8,128)(2,1)} %param.8), kind=kOutput, calls=%fused_computation.16 | convolution fusion | flops 1342308352 | bytes 8388608 | tf_op jit(solution)/shard_map/dot_general | solution.py:34
  196.7 0.3 multiply_reduce_fusion
  197.1 0.6 fusion.32
  197.8 0.3 mul.140
  198.1 0.3 div.77
  198.4 5.8 %fusion.1 = bf16[5120,512]{0,1:T(8,128)(2,1)} fusion(bf16[1,2,256,5120]{3,2,1,0:T(8,128)(2,1)} %param.8, f32[32,8,4,128]{3,2,1,0:T(4,128)S(1)} %bitcast.98, f32[256,512]{1,0:T(8,128)S(1)} %fusion.16, f32[32,8,4,128]{3,2,1,0:T(4,128)S(1)} %bitcast.100, f32[512]{0:T(512)S(1)} %copy-done.5, bf16[1,2,256,512]{3,2,1,0:T(8,128)(2,1)S(1)} %copy-done.2), kind=kOutput, calls=%fused_computation.3 | convolution fusion | flops 1348337664 | bytes 9701376 | tf_op jit(solution)/shard_map/dot_general | solution.py:45
  204.2 8.0 %copy.44 = bf16[5120,512]{1,0:T(8,128)(2,1)} copy(bf16[5120,512]{0,1:T(8,128)(2,1)} %fusion.1) | data formatting | bytes 10485760
  213.0 26.0 %reduce-scatter.14.cloned.1.call-done = bf16[32,320]{1,0:T(8,128)(2,1)} async-done(((bf16[512,320]{1,0:T(8,128)(2,1)}), bf16[32,320]{1,0:T(8,128)(2,1)}) %reduce-scatter.14.cloned.1.call-update) | async-done | bytes 20496
  239.0 1.4 fusion.39
  240.4 37.9 %all_gather.11 = bf16[320,512]{0,1:T(8,128)(2,1)S(1)} all-gather(bf16[320,32]{0,1:T(8,128)(2,1)S(1)} %get-tuple-element.20), channel_id=1, replica_groups=mesh['rep'=16,'fsdp'=16] {'rep'}, dimensions={1}, use_global_device_ids=true | all-gather | bytes 348160 | tf_op jit(solution)/shard_map/all_gather | solution.py:87
  278.5 0.8 fusion.34
  279.3 31.0 %reduce-scatter.12.cloned.1.call-done = bf16[320,512]{1,0:T(8,128)(2,1)} async-done(((bf16[5120,512]{1,0:T(8,128)(2,1)}), bf16[320,512]{1,0:T(8,128)(2,1)}) %reduce-scatter.12.cloned.1.call-update) | async-done | bytes 327696
  310.3 1.2 copy.45
  311.6 0.9 copy.40
  (30 shorter events, 1.4 us)
Async XLA Ops:
  8.0 49.0 %all-gather.6.cloned.1.call-start = ((), (), s32[]{:S(2)}) async-start(), calls=%async_computation.4 | async-start | bytes 5570560 | tf_op jit(solution)/shard_map/all_gather | solution.py:36
  8.7 136.1 %reduce-scatter.10.cloned.1.call-start = ((), (), s32[]{:S(2)}) async-start(), calls=%async_computation.5 | async-start | bytes 5570560
  10.1 52.3 %copy-start.5 = (f32[512]{0:T(512)S(1)}, f32[512]{0:T(512)}, u32[]{:S(2)}) copy-start(f32[512]{0:T(512)} %param.11) | copy-start | bytes 6148
  10.1 53.6 %copy-start.2 = (bf16[1,2,256,512]{3,2,1,0:T(8,128)(2,1)S(1)}, bf16[1,2,256,512]{3,2,1,0:T(8,128)(2,1)}, u32[]{:S(2)}) copy-start(bf16[1,2,256,512]{3,2,1,0:T(8,128)(2,1)} %param.9) | copy-start | bytes 1572868
  77.5 1.0 copy-start
  77.5 69.7 %copy-start.1 = (bf16[1,320,512]{2,1,0:T(8,128)(2,1)S(1)}, bf16[1,320,512]{2,1,0:T(8,128)(2,1)}, u32[]{:S(2)}) copy-start(bf16[1,320,512]{2,1,0:T(8,128)(2,1)} %param.12) | copy-start | bytes 983044
  77.5 114.2 %all-gather.4.cloned.1.call-start = ((), (), s32[]{:S(2)}) async-start(), calls=%async_computation.3 | async-start | bytes 5570560 | tf_op jit(solution)/shard_map/all_gather | solution.py:36
  147.1 91.9 %reduce-scatter.14.cloned.1.call-start = ((), (), s32[]{:S(2)}) async-start(), calls=%async_computation.7 | async-start | bytes 417792
  148.1 162.2 %reduce-scatter.12.cloned.1.call-start = ((), (), s32[]{:S(2)}) async-start(), calls=%async_computation.6 | async-start | bytes 5570560
  212.2 26.8 %copy-start.3 = (f32[320,32]{0,1:T(8,128)S(1)}, f32[320,32]{0,1:T(8,128)}, u32[]{:S(2)}) copy-start(f32[320,32]{0,1:T(8,128)} %param.13) | copy-start | bytes 122884
  212.2 26.8 %copy-start.4 = (f32[320,32]{0,1:T(8,128)S(1)}, f32[320,32]{0,1:T(8,128)}, u32[]{:S(2)}) copy-start(f32[320,32]{0,1:T(8,128)} %param.14) | copy-start | bytes 122884
Sparse Core Ops, SparseCore 0:
  10.8 46.1 all-gather.5
  77.6 67.1 reduce-scatter.9
  147.4 44.1 all-gather.3
Sparse Core Ops, SparseCore 1:
  151.0 87.9 reduce-scatter.13
  241.6 68.7 reduce-scatter.11
where the time goes:
time: 323 us; the launch traced here: 320 us
  waiting for transfers between devices  214 us (66%)
  blocking collectives  37.9 us (12%)
  local copies, waits for them, and re-layouts  24.4 us (8%)
  matrix products  21.2 us (7%)
  between operations  16.2 us (5%)
  other arithmetic  5.72 us (2%)
    unnamed x8, waiting for transfers between devices  124 us
    all_gather x2, waiting for transfers between devices, project_keys(): lax.all_gather(weight_rows, 'fsdp', axis=0, tiled=True)  90.1 us
    all_gather x1, blocking collectives, shards(): lax.all_gather(new_outer.astype(jnp.bfloat16), 'rep', axis=1, tiled=True)  37.9 us
    unnamed x19, local copies, waits for them, and re-layouts  21.3 us
    dot_general x2, matrix products, grad_rows(): lax.dot_general(inputs, key_slope, (((0,), (0,)), ((), ())), preferred_el...  11.6 us
    dot_general x2, matrix products, project_keys(): jnp.dot(inputs, lax.all_gather(weight_rows, 'fsdp', axis=0, tiled=True),...  9.62 us
  transfers between devices with their start and end apart: 5, of which 5 were waited for; matrix products, arithmetic and copies ran while one was open for 8% of the time, Pallas kernels for 0%

commit v1 on v0

v1 whole, which is shorter than its diff:
```python
import functools
import math

import jax
import jax.numpy as jnp
from jax import lax
from jax.experimental import pallas as pl
from jax.experimental.pallas import tpu as pltpu
from jax.sharding import PartitionSpec as P

D = 5120
HD = 128
STEPS = 2
ROUNDS = 64
MOMENTUM_DECAY = 0.9
OUTER_RATE = 0.7
LOCAL_SHARE = 0.25

MESH = pl.DeviceIdType.MESH
F32, BF16 = jnp.float32, jnp.bfloat16
NY, NZ = 4, 2
TOK = 256
ROWS = 320
SHARE = 2 * ROWS
CUT = 384
FR = 80


def add(*terms):
    total = terms[0].astype(F32)
    for term in terms[1:]:
        total = total + term.astype(F32)
    return total


def kernel(
    inner_rate,
    x_hbm,
    c_hbm,
    w_hbm,
    gain_ref,
    f_hbm,
    op_hbm,
    om_hbm,
    plan_ref,
    ow_hbm,
    of_hbm,
    oo_hbm,
    omn_hbm,
    xb,
    cb,
    wg,
    keys,
    slope_t,
    gp,
    gq,
    rp1,
    rp2,
    tpz,
    rp3,
    rq1,
    rq2,
    rq3,
    wout,
    fr,
    opb,
    omb,
    rf1,
    tf2,
    rf2,
    rf3,
    tf4,
    rf4,
    rf5,
    rf6,
    fout,
    oob,
    omnb,
    send_sems,
    recv_sems,
    local_sems,
):
    rep, fs = lax.axis_index("rep"), lax.axis_index("fsdp")
    z, y, c = fs // 8, (fs // 2) % 4, fs % 2
    zh, x = rep // 4, rep % 4
    yp, ym, y2 = (y + 1) % 4, (y + 3) % 4, (y + 2) % 4
    zo, co = 1 - z, 1 - c

    def dev(dz=z, dy=y, dc=c):
        return (rep, dz * 8 + dy * 2 + dc)

    up, down, across, twin = dev(dy=yp), dev(dy=ym), dev(dz=zo), dev(dc=co)
    xs = [(x + d) % 4 for d in (1, 2, 3)]
    zs = [(zh + d) % 4 for d in (1, 2, 3)]
    xdev = [(zh * 4 + i, fs) for i in xs]
    zdev = [(i * 4 + x, fs) for i in zs]

    started, locals_started = [], []

    def send(src, dst, to):
        i = len(started)
        copy = pltpu.make_async_remote_copy(
            src_ref=src,
            dst_ref=dst,
            send_sem=send_sems.at[i],
            recv_sem=recv_sems.at[i],
            device_id=to,
            device_id_type=MESH,
        )
        copy.start()
        started.append(copy)
        return copy

    def local(src, dst):
        copy = pltpu.make_async_copy(src, dst, local_sems.at[len(locals_started)])
        copy.start()
        locals_started.append(copy)
        return copy

    def columns(head):
        return pl.ds(pl.multiple_of(head * HD, HD), HD)

    half = lambda core: pl.ds(pl.multiple_of(core * 2 * HD, 2 * HD), 2 * HD)
    own_rows = pl.ds(pl.multiple_of(c * ROWS, 64), ROWS)
    other_rows = pl.ds(pl.multiple_of(co * ROWS, 64), ROWS)

    w_local = [local(w_hbm.at[0, :, columns(2 * c + h)], wg.at[0, h, z, y, own_rows, :]) for h in range(2)]
    x_local = [local(x_hbm.at[0, 0], xb.at[0, pl.ds(0, TOK), :]), None]
    c_local = [local(c_hbm.at[0, s, :, half(c)], cb.at[s, pl.ds(0, TOK), :]) for s in range(STEPS)]
    x_local[1] = local(x_hbm.at[0, 1], xb.at[1, pl.ds(0, TOK), :])
    f_local = local(f_hbm.at[0], fr)
    op_local = local(op_hbm, opb)
    om_local = local(om_hbm, omb)

    barrier = pltpu.get_barrier_semaphore()
    greeted = [twin, up, down, across] + xdev + zdev
    for to in greeted:
        pl.semaphore_signal(barrier, inc=1, device_id=to, device_id_type=MESH)
    pl.semaphore_wait(barrier, len(greeted))

    w_swap = [
        send(w_hbm.at[0, :, columns(2 * co + h)], wg.at[0, h, z, y, own_rows, :], twin) for h in range(2)
    ]
    x_swap, c_swap = [], []
    for s in range(STEPS):
        x_swap.append(send(x_hbm.at[0, s], xb.at[s, pl.ds(TOK, TOK), :], twin))
        c_swap.append(send(c_hbm.at[0, s, :, half(co)], cb.at[s, pl.ds(TOK, TOK), :], twin))

    class Gather:
        def __init__(self, s, h):
            self.w = wg.at[s, h]

        def block(self, bz, by, at, size):
            return self.w.at[bz, by, pl.ds(at, size), :]

        def push(self, bz, by, at, size, to):
            ref = self.block(bz, by, at, size)
            return send(ref, ref, to)

        def first(self):
            p, q = (0, CUT), (CUT, SHARE - CUT)
            self.pz = self.push(z, y, *p, across)
            self.qu = self.push(z, y, *q, up)
            self.qd = self.push(z, y, *q, down)
            self.pu = self.push(z, y, *p, up)
            self.pd = self.push(z, y, *p, down)
            self.qz = self.push(z, y, *q, across)

        def second(self):
            p, q = (0, CUT), (CUT, SHARE - CUT)
            hp, hq = CUT // 2, (SHARE - CUT) // 2
            self.qu.wait_recv()
            self.quz = self.push(z, ym, *q, across)
            self.quu = self.push(z, ym, CUT, hq, up)
            self.qd.wait_recv()
            self.qdz = self.push(z, yp, *q, across)
            self.qdd = self.push(z, yp, CUT + hq, hq, down)
            self.pz.wait_recv()
            self.pzu = self.push(zo, y, *p, up)
            self.pzd = self.push(zo, y, *p, down)
            self.pu.wait_recv()
            self.puu = self.push(z, ym, 0, hp, up)
            self.pd.wait_recv()
            self.pdd = self.push(z, yp, hp, hp, down)

        def third(self):
            hp, hq = CUT // 2, (SHARE - CUT) // 2
            self.quu.wait_recv()
            self.quuz = self.push(z, y2, CUT, hq, across)
            self.qdd.wait_recv()
            self.qddz = self.push(z, y2, CUT + hq, hq, across)
            self.pzu.wait_recv()
            self.pzuu = self.push(zo, ym, 0, hp, up)
            self.pzd.wait_recv()
            self.pzdd = self.push(zo, yp, hp, hp, down)

        def finish(self):
            for copy in (
                self.qz, self.quz, self.qdz, self.puu, self.pdd,
                self.quuz, self.qddz, self.pzuu, self.pzdd,
            ):
                copy.wait_recv()

    class Scatter:
        def __init__(self, s, h):
            self.s, self.h = s, h
            self.gp, self.gq = gp.at[s, h], gq.at[s, h]
            self.rp1, self.rp2, self.rp3 = rp1.at[s, h], rp2.at[s, h], rp3.at[s, h]
            self.tpz = tpz.at[s, h]
            self.rq1, self.rq2, self.rq3 = rq1.at[s, h], rq2.at[s, h], rq3.at[s, h]

        def grad(self, by):
            lhs = slope_t[self.h]

            def one(bz, carry):
                at = pl.multiple_of((bz * NY + by) * SHARE, HD)
                part = jnp.dot(lhs, xb[self.s, :, pl.ds(at, SHARE)], preferred_element_type=F32)
                self.gp[bz, by] = part[:, :CUT].astype(BF16)
                self.gq[bz, by] = part[:, CUT:].astype(BF16)
                return carry

            lax.fori_loop(0, NZ, one, 0)

        def first(self):
            lo, hi = pl.ds(0, HD // 2), pl.ds(HD // 2, HD // 2)
            self.grad(y2)
            self.z2 = send(self.gq.at[zo, y2], self.rq1.at[y2], across)
            self.pu = send(self.gp.at[:, y2, lo], self.rp1.at[0], up)
            self.pd = send(self.gp.at[:, y2, hi], self.rp1.at[1], down)
            self.grad(yp)
            self.zp = send(self.gq.at[zo, yp], self.rq1.at[yp], across)
            self.pu1 = send(self.gp.at[:, yp, hi], self.rp2.at[0, :, hi], up)
            self.grad(ym)
            self.zm = send(self.gq.at[zo, ym], self.rq1.at[ym], across)
            self.pd1 = send(self.gp.at[:, ym, lo], self.rp2.at[1, :, lo], down)
            self.grad(y)
            self.z0 = send(self.gq.at[zo, y], self.rq1.at[y], across)

        def second(self):
            lo, hi = pl.ds(0, HD // 2), pl.ds(HD // 2, HD // 2)
            self.z2.wait_recv()
            self.rq1[y2] = add(self.rq1[y2], self.gq[z, y2]).astype(BF16)
            self.qu = send(self.rq1.at[y2, lo], self.rq2.at[0], up)
            self.qd = send(self.rq1.at[y2, hi], self.rq2.at[1], down)
            self.pu.wait_recv()
            self.rp1[0] = add(self.rp1[0], self.gp[:, yp, lo]).astype(BF16)
            self.pu2 = send(self.rp1.at[0], self.rp2.at[0, :, lo], up)
            self.pd.wait_recv()
            self.rp1[1] = add(self.rp1[1], self.gp[:, ym, hi]).astype(BF16)
            self.pd2 = send(self.rp1.at[1], self.rp2.at[1, :, hi], down)
            self.zp.wait_recv()
            self.rq1[yp] = add(self.rq1[yp], self.gq[z, yp]).astype(BF16)
            self.qu1 = send(self.rq1.at[yp, hi], self.rq3.at[0, hi], up)
            self.zm.wait_recv()
            self.rq1[ym] = add(self.rq1[ym], self.gq[z, ym]).astype(BF16)
            self.qd1 = send(self.rq1.at[ym, lo], self.rq3.at[1, lo], down)

        def third(self):
            lo, hi = pl.ds(0, HD // 2), pl.ds(HD // 2, HD // 2)
            self.qu.wait_recv()
            self.rq1[yp, lo] = add(self.rq1[yp, lo], self.rq2[0]).astype(BF16)
            self.qu2 = send(self.rq1.at[yp, lo], self.rq3.at[0, lo], up)
            self.qd.wait_recv()
            self.rq1[ym, hi] = add(self.rq1[ym, hi], self.rq2[1]).astype(BF16)
            self.qd2 = send(self.rq1.at[ym, hi], self.rq3.at[1, hi], down)
            for copy in (self.pu1, self.pu2, self.pd1, self.pd2):
                copy.wait_recv()
            self.tpz[...] = add(self.gp[zo, y], self.rp2[0, zo], self.rp2[1, zo]).astype(BF16)
            self.zl = send(self.tpz, self.rp3, across)

        def finish(self):
            self.z0.wait_recv()
            for copy in (self.qu1, self.qu2, self.qd1, self.qd2):
                copy.wait_recv()
            q = add(self.gq[z, y], self.rq1[y], self.rq3[0], self.rq3[1])
            old = wg.at[self.s, self.h, z, y]
            new = wg.at[1, self.h, z, y] if self.s + 1 < STEPS else wout.at[self.h]
            scale = inner_rate * D**-0.5
            new[CUT:, :] = (old[CUT:, :].astype(F32) - scale * q.T).astype(BF16)
            self.zl.wait_recv()
            p = add(self.gp[z, y], self.rp2[0, z], self.rp2[1, z], self.rp3[...])
            new[:CUT, :] = (old[:CUT, :].astype(F32) - scale * p.T).astype(BF16)

    def project(s, h):
        def one(i, carry):
            at = pl.multiple_of(i * 2 * SHARE, HD)
            lhs = xb[s, :, pl.ds(at, 2 * SHARE)]
            bz, by = i // 2, 2 * (i % 2)
            rhs = wg[s, h, bz, pl.ds(by, 2)].reshape(2 * SHARE, HD)
            part = jnp.dot(lhs, rhs, preferred_element_type=F32)
            keys[...] = jnp.where(i == 0, part, keys[...] + part)
            return carry

        lax.fori_loop(0, NY * NZ // 2, one, 0)

    def backward(s, h):
        k = keys[...] * D**-0.5
        inverse = lax.rsqrt(jnp.mean(k * k, axis=-1, keepdims=True) + 1e-06)
        u = k * inverse
        gain = gain_ref[pl.ds(2 * c + h, 1), :]
        pulled = cb[s, :, h * HD : (h + 1) * HD].astype(F32) * gain
        slope = (pulled - u * jnp.mean(pulled * u, axis=-1, keepdims=True)) * inverse
        slope_t[h] = slope.T.astype(BF16)

    outer = {}

    def outer_0():
        outer["a"] = [send(f_hbm.at[0, pl.ds(pl.multiple_of(i * FR, 16), FR), :], rf1.at[n], to)
                      for n, (i, to) in enumerate(zip(xs, xdev))]

    def outer_1():
        f_local.wait()
        for copy in outer["a"]:
            copy.wait_recv()
        mine = fr[pl.ds(pl.multiple_of(x * FR, 16), FR), :]
        total = add(mine, rf1[0], rf1[1], rf1[2]).astype(BF16)
        for i in range(4):
            tf2[i] = total[:, i * HD : (i + 1) * HD]
        outer["b"] = [send(tf2.at[i], rf2.at[n], to) for n, (i, to) in enumerate(zip(zs, zdev))]

    def outer_2():
        for copy in outer["b"]:
            copy.wait_recv()
        rf3[x] = add(tf2[zh], rf2[0], rf2[1], rf2[2])
        outer["c"] = [send(rf3.at[x], rf3.at[x], to) for to in xdev]

    def outer_3():
        op_local.wait()
        om_local.wait()
        for copy in outer["c"]:
            copy.wait_recv()
        lane = lax.broadcasted_iota(jnp.int32, (FR, HD), 1)
        plan = jnp.full((8, HD), plan_ref[0].astype(F32))
        factor = (OUTER_RATE * (0.55 + 0.45 * jnp.cos(math.pi * plan / ROUNDS)))[:1]
        pick = lambda a: jnp.where(
            x < 2,
            jnp.where(x == 0, a[:, 0:32], a[:, 32:64]),
            jnp.where(x == 2, a[:, 64:96], a[:, 96:128]),
        )
        for i in range(4):
            rows = slice(i * FR, (i + 1) * FR)
            old = jnp.concatenate([opb[rows, :]] * 4, axis=1)
            moment = jnp.concatenate([omb[rows, :]] * 4, axis=1)
            pseudo = old - rf3[i] * (1.0 / 16)
            moment = MOMENTUM_DECAY * moment + pseudo
            new = old - factor * (pseudo + MOMENTUM_DECAY * moment)
            oob[rows, :] = pick(new)
            omnb[rows, :] = pick(moment)
            tf4[i] = jnp.where(lane // 32 == x, new, 0.0).astype(BF16)
        local(oob, oo_hbm)
        local(omnb, omn_hbm)
        outer["d"] = [send(tf4.at[i], rf4.at[n], to) for n, (i, to) in enumerate(zip(xs, xdev))]

    def outer_4():
        for copy in outer["d"]:
            copy.wait_recv()
        rf5[zh] = add(tf4[x], rf4[0], rf4[1], rf4[2]).astype(BF16)
        outer["e"] = [send(rf5.at[zh], rf5.at[zh], to) for to in zdev]

    def outer_5():
        for copy in outer["e"]:
            copy.wait_recv()
        outer["f"] = [send(rf5, rf6.at[x], to) for to in xdev]
        rf6[x] = rf5[...]

    def outer_6():
        for copy in outer["f"]:
            copy.wait_recv()
        for i in range(4):
            for j in range(4):
                rows, cols = slice(i * FR, (i + 1) * FR), slice(j * HD, (j + 1) * HD)
                blend = LOCAL_SHARE * fr[rows, cols].astype(F32)
                blend = blend + (1.0 - LOCAL_SHARE) * rf6[i, j].astype(F32)
                fout[rows, cols] = blend.astype(BF16)
        local(fout, of_hbm.at[0])

    def write(h):
        src = wout.at[h]
        local(src.at[own_rows, :], ow_hbm.at[0, :, columns(2 * c + h)])
        return send(src.at[other_rows, :], ow_hbm.at[0, :, columns(2 * c + h)], twin)

    ga, gb = [Gather(s, 0) for s in range(2)], [Gather(s, 1) for s in range(2)]
    sa, sb = [Scatter(s, 0) for s in range(2)], [Scatter(s, 1) for s in range(2)]

    w_local[0].wait()
    w_swap[0].wait_recv()
    ga[0].first()
    outer_0()
    w_local[1].wait()
    w_swap[1].wait_recv()
    ga[0].second()
    gb[0].first()
    ga[0].third()
    outer_1()
    gb[0].second()
    for s in range(STEPS):
        x_local[s].wait()
        x_swap[s].wait_recv()
        c_local[s].wait()
        c_swap[s].wait_recv()
        ga[s].finish()
        project(s, 0)
        backward(s, 0)
        gb[s].third()
        sa[s].first()
        outer_2() if s == 0 else outer_5()
        sa[s].second()
        gb[s].finish()
        project(s, 1)
        backward(s, 1)
        sa[s].third()
        sb[s].first()
        outer_3() if s == 0 else outer_6()
        sa[s].finish()
        if s == 0:
            ga[1].first()
            sb[0].second()
            ga[1].second()
            sb[0].third()
            ga[1].third()
            outer_4()
            sb[0].finish()
            gb[1].first()
            gb[1].second()
        else:
            out_a = write(0)
            sb[1].second()
            sb[1].third()
            sb[1].finish()
            out_b = write(1)
    out_a.wait_recv()
    out_b.wait_recv()
    for copy in locals_started[9:]:
        copy.wait()
    for copy in started:
        copy.wait_send()


def shards(
    layer_input, cotangent, key_weight, key_gain, fragment, outer_params, outer_momentum, plan
):
    tokens = layer_input.shape[2] * lax.axis_size("fsdp")
    inner_rate = 0.5 * math.sqrt(D / tokens)
    any_spec = pl.BlockSpec(memory_space=pl.ANY)
    vmem = lambda *shape, dtype=BF16: pltpu.VMEM(shape, dtype)
    hc, zr = HD // 2, SHARE - CUT
    return pl.pallas_call(
        functools.partial(kernel, inner_rate),
        out_shape=(
            jax.ShapeDtypeStruct(key_weight.shape, BF16),
            jax.ShapeDtypeStruct(fragment.shape, BF16),
            jax.ShapeDtypeStruct(outer_params.shape, F32),
            jax.ShapeDtypeStruct(outer_momentum.shape, F32),
        ),
        in_specs=[any_spec] * 3
        + [pl.BlockSpec(memory_space=pltpu.VMEM)]
        + [any_spec] * 3
        + [pl.BlockSpec(memory_space=pltpu.SMEM)],
        out_specs=[any_spec] * 4,
        scratch_shapes=[
            vmem(STEPS, 2 * TOK, D),
            vmem(STEPS, 2 * TOK, 2 * HD),
            vmem(STEPS, 2, NZ, NY, SHARE, HD),
            vmem(2 * TOK, HD, dtype=F32),
            vmem(2, HD, 2 * TOK),
            vmem(STEPS, 2, NZ, NY, HD, CUT),
            vmem(STEPS, 2, NZ, NY, HD, zr),
            vmem(STEPS, 2, 2, NZ, hc, CUT),
            vmem(STEPS, 2, 2, NZ, HD, CUT),
            vmem(STEPS, 2, HD, CUT),
            vmem(STEPS, 2, HD, CUT),
            vmem(STEPS, 2, NY, HD, zr),
            vmem(STEPS, 2, 2, hc, zr),
            vmem(STEPS, 2, 2, HD, zr),
            vmem(2, SHARE, HD),
            vmem(ROWS, 4 * HD),
            vmem(ROWS, 32, dtype=F32),
            vmem(ROWS, 32, dtype=F32),
            vmem(3, FR, 4 * HD),
            vmem(4, FR, HD),
            vmem(3, FR, HD),
            vmem(4, FR, HD, dtype=F32),
            vmem(4, FR, HD),
            vmem(3, FR, HD),
            vmem(4, FR, HD),
            vmem(4, 4, FR, HD),
            vmem(ROWS, 4 * HD),
            vmem(ROWS, 32, dtype=F32),
            vmem(ROWS, 32, dtype=F32),
            pltpu.SemaphoreType.DMA((180,)),
            pltpu.SemaphoreType.DMA((180,)),
            pltpu.SemaphoreType.DMA((16,)),
        ],
        compiler_params=pltpu.CompilerParams(
            collective_id=0, has_side_effects=True, vmem_limit_bytes=56 << 20
        ),
        cost_estimate=pl.CostEstimate(
            flops=4 * 2 * 256 * D * 512, bytes_accessed=8 << 20, transcendentals=0
        ),
    )(
        layer_input,
        cotangent,
        key_weight,
        key_gain.reshape(4, HD),
        fragment,
        outer_params,
        outer_momentum,
        plan,
    )


def solution(mesh):
    placed = (
        P("rep", None, "fsdp", None),
        P("rep", None, "fsdp", None),
        P("rep", "fsdp", None),
        P(),
        P("rep", "fsdp", None),
        P("fsdp", "rep"),
        P("fsdp", "rep"),
        P(),
    )
    return jax.shard_map(
        shards,
        mesh=mesh,
        in_specs=placed,
        out_specs=(
            P("rep", "fsdp", None),
            P("rep", "fsdp", None),
            P("fsdp", "rep"),
            P("fsdp", "rep"),
        ),
        check_vma=False,
    )
```

time: 323 us -> 109 us (0.34)
  waiting for transfers between devices: 214 us -> 0 us
  Pallas kernels: 0 us -> 97.6 us
  blocking collectives: 37.9 us -> 0 us
  matrix products: 21.2 us -> 0 us
  between operations: 16.2 us -> 1.29 us
  local copies, waits for them, and re-layouts: 24.4 us -> 9.88 us
  other arithmetic: 5.72 us -> 0 us
    unnamed x8 -> x0, waiting for transfers between devices: 124 us -> none
    pallas_call x0 -> x1, Pallas kernels: none -> 97.6 us  [shards(): pl.pallas_call(functools.partial(kernel, inner_rate), out_shape=(jax.Shap...]
    all_gather x2 -> x0, waiting for transfers between devices: 90.1 us -> none  [project_keys(): lax.all_gather(weight_rows, 'fsdp', axis=0, tiled=True)]
    all_gather x1 -> x0, blocking collectives: 37.9 us -> none  [shards(): lax.all_gather(new_outer.astype(jnp.bfloat16), 'rep', axis=1, tiled=True)]
    dot_general x4 -> x0, matrix products: 21.2 us -> none  [the longest x2 11.6 us: grad_rows(): lax.dot_general(inputs, key_slope, (((0,), (0,)), ((), ())), preferred_el...]
    unnamed x19 -> x4, local copies, waits for them, and re-layouts: 21.3 us -> 6.6 us
    pallas_call x0 -> x2, local copies, waits for them, and re-layouts: none -> 3.29 us  [shards(): pl.pallas_call(functools.partial(kernel, inner_rate), out_shape=(jax.Shap...]
  transfers between devices with their start and end apart: 5 -> 0, of which waited for: 5 -> 0; matrix products, arithmetic and copies ran while one was open for 8% -> 0% of each run, Pallas kernels for 0% -> 0%
where the time goes in v1:
time: 109 us
  Pallas kernels  97.6 us (90%)
  local copies, waits for them, and re-layouts  9.88 us (9%)
  between operations  1.29 us (1%)
    pallas_call x1, Pallas kernels, shards(): pl.pallas_call(functools.partial(kernel, inner_rate), out_shape=(jax.Shap...  97.6 us
    unnamed x4, local copies, waits for them, and re-layouts  6.6 us
    pallas_call x2, local copies, waits for them, and re-layouts, shards(): pl.pallas_call(functools.partial(kernel, inner_rate), out_shape=(jax.Shap...  3.29 us

profile of v1, /device:TPU:1, one launch (start us, length us, event | category | flops | bytes accessed | tf_op | source)
XLA Modules:
  0.0 108.7 jit_solution(1382148903477792324)
XLA Ops:
  1.3 1.6 %copy.12.op_hbm = f32[320,32]{1,0:T(8,128)} copy(f32[320,32]{0,1:T(8,128)} %param.13) | data formatting | bytes 81920 | tf_op args[5]
  2.9 1.6 %copy.13.om_hbm = f32[320,32]{1,0:T(8,128)} copy(f32[320,32]{0,1:T(8,128)} %param.14) | data formatting | bytes 81920 | tf_op args[6]
  4.4 97.6 %shard_map.111 = (bf16[1,320,512]{2,1,0:T(8,128)(2,1)}, bf16[1,320,512]{2,1,0:T(8,128)(2,1)}, f32[320,32]{1,0:T(8,128)}, f32[320,32]{1,0:T(8,128)}) custom-call(bf16[1,2,256,5120]{3,2,1,0:T(8,128)(2,1)} %x_hbm.1, bf16[1,2,256,512]{3,2,1,0:T(8,128)(2,1)} %c_hbm.1, bf16[1,320,512]{2,1,0:T(8,128)(2,1)} %w_hbm.1, f32[4,128]{1,0:T(4,128)} %bitcast.1, ...), custom_call_target="tpu_custom_call" | custom-call | flops 5368709120 | bytes 8388608 | tf_op jit(solution)/shard_map/pallas_call | solution.py:447
  102.0 1.6 %copy.14 = f32[320,32]{0,1:T(8,128)} copy(f32[320,32]{1,0:T(8,128)} %get-tuple-element.6) | data formatting | bytes 81920 | tf_op jit(solution)/shard_map/pallas_call | solution.py:447
  103.7 1.6 %copy.15 = f32[320,32]{0,1:T(8,128)} copy(f32[320,32]{1,0:T(8,128)} %get-tuple-element.7) | data formatting | bytes 81920 | tf_op jit(solution)/shard_map/pallas_call | solution.py:447
  105.3 1.7 %copy.19 = bf16[1,320,512]{2,1,0:T(8,128)(2,1)} copy(bf16[1,320,512]{2,1,0:T(8,128)(2,1)} %get-tuple-element.12) | data formatting | bytes 655360
  107.0 1.7 %copy.20 = bf16[1,320,512]{2,1,0:T(8,128)(2,1)} copy(bf16[1,320,512]{2,1,0:T(8,128)(2,1)} %get-tuple-element.13) | data formatting | bytes 655360

commit v2 on v0

v2 whole, which is shorter than its diff:
```python
import functools
import math

import jax
import jax.numpy as jnp
from jax import lax
from jax.experimental import pallas as pl
from jax.experimental.pallas import tpu as pltpu
from jax.sharding import PartitionSpec as P

D = 5120
HD = 128
STEPS = 2
ROUNDS = 64
MOMENTUM_DECAY = 0.9
OUTER_RATE = 0.7
LOCAL_SHARE = 0.25

ORDER = (
    51, 1, 2, 0, 50, 200, 52, 4, 3, 5, 55, 7, 54, 201, 9, 6, 53, 11, 57, 12,
    10, 8, 62, 61, 56, 63, 13, 14, 60, 59, 58, 15, 16, 17, 64, 18, 65, 66, 20, 22,
    68, 21, 69, 19, 67, 24, 202, 26, 23, 25, 74, 70, 27, 72, 71, 73, 28, 101, 102, 75,
    76, 29, 100, 203, 77, 104, 103, 78, 151, 105, 107, 106, 112, 79, 150, 108, 109, 111, 110, 152,
    204, 153, 154, 113, 114, 155, 157, 156, 162, 115, 116, 158, 159, 163, 160, 161, 118, 117, 164, 122,
    121, 165, 166, 120, 119, 167, 168, 205, 170, 172, 171, 127, 124, 169, 174, 123, 125, 126, 173, 177,
    176, 175, 206, 128, 129, 130, 178, 179, 180,
)

MESH = pl.DeviceIdType.MESH
F32, BF16 = jnp.float32, jnp.bfloat16
NY, NZ = 4, 2
TOK = 256
ROWS = 320
SHARE = 2 * ROWS
CUT = 384
TOP = 384
SENT, CAME = 15, 55
FR = 80


def add(*terms):
    total = terms[0].astype(F32)
    for term in terms[1:]:
        total = total + term.astype(F32)
    return total


def kernel(
    inner_rate,
    x_hbm,
    c_hbm,
    w_hbm,
    gain_hbm,
    f_hbm,
    op_hbm,
    om_hbm,
    plan_hbm,
    ow_hbm,
    of_hbm,
    oo_hbm,
    omn_hbm,
    xb,
    cb,
    wg,
    keys,
    slope_t,
    gp,
    gq,
    rp1,
    rp2,
    tpz,
    rp3,
    rq1,
    rq2,
    rq3,
    wout,
    fr,
    opb,
    omb,
    rf1,
    tf2,
    rf2,
    rf3,
    tf4,
    rf4,
    rf5,
    rf6,
    fout,
    oob,
    omnb,
    side,
    gain_ref,
    plan_ref,
    relay,
    send_sems,
    recv_sems,
    local_sems,
):
    rep, fs = lax.axis_index("rep"), lax.axis_index("fsdp")
    z, y, c = fs // 8, (fs // 2) % 4, fs % 2
    zh, x = rep // 4, rep % 4
    yp, ym, y2 = (y + 1) % 4, (y + 3) % 4, (y + 2) % 4
    zo, co = 1 - z, 1 - c

    def dev(dz=z, dy=y, dc=c):
        return (rep, dz * 8 + dy * 2 + dc)

    up, down, across, twin = dev(dy=yp), dev(dy=ym), dev(dz=zo), dev(dc=co)
    xs = [(x + d) % 4 for d in (1, 2, 3)]
    zs = [(zh + d) % 4 for d in (1, 2, 3)]
    xdev = [(zh * 4 + i, fs) for i in xs]
    zdev = [(i * 4 + x, fs) for i in zs]

    locals_started, came_at, sent_at = [], {}, {}

    def remote(src, dst, sent, came, to=twin):
        return pltpu.make_async_remote_copy(
            src_ref=src,
            dst_ref=dst,
            send_sem=send_sems.at[sent_at.setdefault(sent, len(sent_at))],
            recv_sem=recv_sems.at[came_at.setdefault(came, len(came_at))],
            device_id=to,
            device_id_type=MESH,
        )

    def send(src, dst, to, sent, came):
        remote(src, dst, sent, came, to).start()

    def landed(ref, came):
        remote(ref, ref, "x0", came).wait_recv()

    def left(ref, sent):
        remote(ref, ref, sent, "x0").wait_send()

    def local(src, dst):
        copy = pltpu.make_async_copy(src, dst, local_sems.at[len(locals_started)])
        copy.start()
        locals_started.append(copy)
        return copy

    def columns(head):
        return pl.ds(pl.multiple_of(head * HD, HD), HD)

    half = lambda core: pl.ds(pl.multiple_of(core * 2 * HD, 2 * HD), 2 * HD)
    own_rows = pl.ds(pl.multiple_of(c * ROWS, 64), ROWS)
    other_rows = pl.ds(pl.multiple_of(co * ROWS, 64), ROWS)

    barrier = pltpu.get_barrier_semaphore()
    plane = [(rep, z * 8 + yp * 2), (rep, z * 8 + ym * 2), (rep, zo * 8 + y * 2)]
    plane += [(zh * 4 + i, z * 8 + y * 2) for i in xs]
    depth = [(i * 4 + x, z * 8 + y * 2 + 1) for i in zs]
    for to in plane + depth:
        pl.semaphore_signal(barrier, inc=1, device_id=to, device_id_type=MESH)

    @pl.when(c == 1)
    def _():
        pl.semaphore_signal(barrier, inc=1, device_id=twin, device_id_type=MESH)

    w_local = [local(w_hbm.at[0, :, columns(2 * c + h)], wg.at[0, h, z, y, own_rows, :]) for h in range(2)]
    x_local = [local(x_hbm.at[0, 0], xb.at[0, pl.ds(0, TOK), :]), None]
    c_local = [local(c_hbm.at[0, s, :, half(c)], cb.at[s, pl.ds(0, TOK), :]) for s in range(STEPS)]
    x_local[1] = local(x_hbm.at[0, 1], xb.at[1, pl.ds(0, TOK), :])
    f_local = local(f_hbm.at[0], fr)
    op_local = local(op_hbm, opb)
    om_local = local(om_hbm, omb)
    gain_local = local(gain_hbm, gain_ref)
    plan_local = local(plan_hbm, plan_ref)

    @pl.when(c == 0)
    def _():
        pl.semaphore_wait(barrier, 2 * len(plane) + 1)
        pl.semaphore_signal(relay, inc=1, device_id=twin, device_id_type=MESH)

    @pl.when(c == 1)
    def _():
        pl.semaphore_wait(relay, 1)

    def meet_depth():
        @pl.when(c == 1)
        def _():
            pl.semaphore_wait(barrier, 2 * len(depth))
            pl.semaphore_signal(relay, inc=1, device_id=twin, device_id_type=MESH)

        @pl.when(c == 0)
        def _():
            pl.semaphore_wait(relay, 1)

    for h in range(2):
        dst = wg.at[0, h, z, y, own_rows, :]
        send(w_hbm.at[0, :, columns(2 * co + h)], dst, twin, "ws", "ws")
    send(x_hbm.at[0, 0], xb.at[0, pl.ds(TOK, TOK), :], twin, "x0", "x0")
    for s in range(STEPS):
        send(c_hbm.at[0, s, :, half(co)], cb.at[s, pl.ds(TOK, TOK), :], twin, "c", "c")
    send(x_hbm.at[0, 1], xb.at[1, pl.ds(TOK, TOK), :], twin, "x1", "x1")

    todo = {}
    lo, hi = pl.ds(0, HD // 2), pl.ds(HD // 2, HD // 2)
    groups = dict(puu="k3", pdd="k3", qdz="k3", quz="k4", quuz="k4", qddz="k4", pzuu="k4", pzdd="k4",
                  Pu1="rp", Pu2="rp", Pd1="rp", Pd2="rp", z0="uq", Qu1="uq", Qu2="uq", Qd1="uq", Qd2="uq")

    def inner(s, h):
        k, mine = "AB"[h], "AB"[h] + str(s)
        w, sl = wg.at[s, h], slope_t.at[h]
        mp, mq = gp.at[s, h], gq.at[s, h]
        p1, p2, p3, pz = rp1.at[s, h], rp2.at[s, h], rp3.at[s, h], tpz.at[s, h]
        q1, q2, q3 = rq1.at[s, h], rq2.at[s, h], rq3.at[s, h]
        acc = keys.at[h]
        first, rest = (0, TOP), (TOP, SHARE - TOP)
        hp, hq = TOP // 2, (SHARE - TOP) // 2

        def push(name, bz, by, at, size, to):
            ref = w.at[bz, by, pl.ds(at, size), :]
            send(ref, ref, to, mine, k + groups.get(name, name))

        def put(name, src, dst, to):
            send(src, dst, to, mine, k + groups.get(name, name))

        def take(name, ref):
            landed(ref, k + name)

        def rows(at, size):
            return w.at[z, y, pl.ds(at, size), :]

        def g_p():
            push("pz", z, y, *first, across)
            push("pu", z, y, *first, up)
            push("pd", z, y, *first, down)

        def g_q():
            push("qu", z, y, *rest, up)
            push("qd", z, y, *rest, down)

        def g_z():
            push("qz", z, y, *rest, across)

        def a_qu():
            take("qu", rows(*rest))
            push("quu", z, ym, TOP, hq, up)
            push("quz", z, ym, *rest, across)

        def a_qd():
            take("qd", rows(*rest))
            push("qdd", z, yp, TOP + hq, hq, down)
            push("qdz", z, yp, *rest, across)

        def a_pz():
            take("pz", rows(*first))
            push("pzu", zo, y, *first, up)
            push("pzd", zo, y, *first, down)

        def a_pu():
            take("pu", rows(*first))
            push("puu", z, ym, 0, hp, up)

        def a_pd():
            take("pd", rows(*first))
            push("pdd", z, yp, hp, hp, down)

        def a_quu():
            take("quu", rows(TOP, hq))
            push("quuz", z, y2, TOP, hq, across)

        def a_qdd():
            take("qdd", rows(TOP, hq))
            push("qddz", z, y2, TOP + hq, hq, across)

        def a_pzu():
            take("pzu", rows(*first))
            push("pzuu", zo, ym, 0, hp, up)

        def a_pzd():
            take("pzd", rows(*first))
            push("pzdd", zo, yp, hp, hp, down)

        def project(*blocks):
            at = [pl.ds(pl.multiple_of((bz * NY + by) * SHARE, HD), SHARE) for bz, by in blocks]
            lhs = jnp.concatenate([xb[s, :, cols] for cols in at], axis=1)
            rhs = jnp.concatenate([w[bz, by] for bz, by in blocks], axis=0)
            return jnp.dot(lhs, rhs, preferred_element_type=F32)

        def k1():
            if h == 0:
                x_local[s].wait()
                landed(xb.at[s, pl.ds(TOK, TOK), :], "x" + str(s))
            acc[...] = project((z, y), (z, yp))

        def k2():
            take("qz", rows(*rest))
            acc[...] += project((z, ym), (zo, y))

        def k3():
            take("k3", w.at[z, y])
            acc[...] += project((z, y2), (zo, yp))

        def k4():
            take("k4", cb.at[0, pl.ds(0, (2 * SHARE - TOP) // 2), :])
            if h == 0 and s == 0:
                c_local[0].wait()
                c_local[1].wait()
                landed(cb.at[0], "c")
                gain_local.wait()
            kv = (acc[...] + project((zo, ym), (zo, y2))) * D**-0.5
            inverse = lax.rsqrt(jnp.mean(kv * kv, axis=-1, keepdims=True) + 1e-06)
            u = kv * inverse
            gain = gain_ref[pl.ds(2 * c + h, 1), :]
            pulled = cb[s, :, h * HD : (h + 1) * HD].astype(F32) * gain
            slope = (pulled - u * jnp.mean(pulled * u, axis=-1, keepdims=True)) * inverse
            sl[...] = slope.T.astype(BF16)

        def grad(by):
            lhs = sl[...]

            def one(bz, carry):
                at = pl.multiple_of((bz * NY + by) * SHARE, HD)
                part = jnp.dot(lhs, xb[s, :, pl.ds(at, SHARE)], preferred_element_type=F32)
                mp[bz, by] = part[:, :CUT].astype(BF16)
                mq[bz, by] = part[:, CUT:].astype(BF16)
                return carry

            lax.fori_loop(0, NZ, one, 0)

        def g2():
            grad(y2)
            put("z2", mq.at[zo, y2], q1.at[y2], across)
            put("Pu", mp.at[:, y2, lo], p1.at[0], up)
            put("Pd", mp.at[:, y2, hi], p1.at[1], down)

        def gu():
            grad(yp)
            put("zp", mq.at[zo, yp], q1.at[yp], across)
            put("Pu1", mp.at[:, yp, hi], p2.at[0, :, hi], up)

        def gd():
            grad(ym)
            put("zm", mq.at[zo, ym], q1.at[ym], across)
            put("Pd1", mp.at[:, ym, lo], p2.at[1, :, lo], down)

        def g0():
            grad(y)
            put("z0", mq.at[zo, y], q1.at[y], across)

        def r_z2():
            take("z2", q1.at[y2])
            q1[y2] = add(q1[y2], mq[z, y2]).astype(BF16)
            put("Qu", q1.at[y2, lo], q2.at[0], up)
            put("Qd", q1.at[y2, hi], q2.at[1], down)

        def r_pu():
            take("Pu", p1.at[0])
            p1[0] = add(p1[0], mp[:, yp, lo]).astype(BF16)
            put("Pu2", p1.at[0], p2.at[0, :, lo], up)

        def r_pd():
            take("Pd", p1.at[1])
            p1[1] = add(p1[1], mp[:, ym, hi]).astype(BF16)
            put("Pd2", p1.at[1], p2.at[1, :, hi], down)

        def r_zp():
            take("zp", q1.at[yp])
            q1[yp] = add(q1[yp], mq[z, yp]).astype(BF16)
            put("Qu1", q1.at[yp, hi], q3.at[0, hi], up)

        def r_zm():
            take("zm", q1.at[ym])
            q1[ym] = add(q1[ym], mq[z, ym]).astype(BF16)
            put("Qd1", q1.at[ym, lo], q3.at[1, lo], down)

        def r_qu():
            take("Qu", q2.at[0])
            q1[yp, lo] = add(q1[yp, lo], q2[0]).astype(BF16)
            put("Qu2", q1.at[yp, lo], q3.at[0, lo], up)

        def r_qd():
            take("Qd", q2.at[1])
            q1[ym, hi] = add(q1[ym, hi], q2[1]).astype(BF16)
            put("Qd2", q1.at[ym, hi], q3.at[1, hi], down)

        def r_p():
            take("rp", p2)
            pz[...] = add(mp[zo, y], p2[0, zo], p2[1, zo]).astype(BF16)
            put("zl", pz, p3, across)

        old = w.at[z, y]
        new = wg.at[1, h, z, y] if s + 1 < STEPS else wout.at[h]
        scale = inner_rate * D**-0.5

        def uq():
            take("uq", q1.at[pl.ds(0, 3)])
            total = add(mq[z, y], q1[y], q3[0], q3[1])
            new[CUT:, :] = (old[CUT:, :].astype(F32) - scale * total.T).astype(BF16)

        def up_():
            take("zl", p3)
            total = add(mp[z, y], p2[0, z], p2[1, z], p3[...])
            new[:CUT, :] = (old[:CUT, :].astype(F32) - scale * total.T).astype(BF16)

        def write():
            src, cols = wout.at[h], columns(2 * c + h)
            local(src.at[own_rows, :], ow_hbm.at[0, :, cols])
            send(src.at[other_rows, :], ow_hbm.at[0, :, cols], twin, "w", "w")

        steps = dict(
            gp=g_p, gq=g_q, gz=g_z, a_qu=a_qu, a_qd=a_qd, a_pz=a_pz, a_pu=a_pu, a_pd=a_pd,
            a_quu=a_quu, a_qdd=a_qdd, a_pzu=a_pzu, a_pzd=a_pzd, k1=k1, k2=k2, k3=k3, k4=k4,
            g2=g2, gu=gu, gd=gd, g0=g0, r_z2=r_z2, r_pu=r_pu, r_pd=r_pd, r_zp=r_zp, r_zm=r_zm,
            r_qu=r_qu, r_qd=r_qd, r_p=r_p, uq=uq, up=up_, w=write,
        )
        for i, step in enumerate(steps.values()):
            todo[100 * s + 50 * h + i] = step

    for s in range(STEPS):
        for h in range(2):
            inner(s, h)

    def outer_0():
        for n, (i, to) in enumerate(zip(xs, xdev)):
            src = f_hbm.at[0, pl.ds(pl.multiple_of(i * FR, 16), FR), :]
            send(src, rf1.at[n], to, "a", "a")

    def outer_1():
        f_local.wait()
        landed(rf1, "a")
        mine = fr[pl.ds(pl.multiple_of(x * FR, 16), FR), :]
        total = add(mine, rf1[0], rf1[1], rf1[2]).astype(BF16)
        for i in range(4):
            tf2[i] = total[:, i * HD : (i + 1) * HD]
        meet_depth()
        for n, (i, to) in enumerate(zip(zs, zdev)):
            send(tf2.at[i], rf2.at[n], to, "b", "b")

    def outer_2():
        landed(rf2, "b")
        rf3[x] = add(tf2[zh], rf2[0], rf2[1], rf2[2])
        for to in xdev:
            send(rf3.at[x], rf3.at[x], to, "g", "g")

    def outer_3():
        op_local.wait()
        om_local.wait()
        plan_local.wait()
        landed(rf3.at[pl.ds(0, 3)], "g")
        plan = jnp.full((8, HD), plan_ref[0].astype(F32))
        factor = (OUTER_RATE * (0.55 + 0.45 * jnp.cos(math.pi * plan / ROUNDS)))[:1, :1]
        mine = pl.ds(pl.multiple_of(x * 32, 32), 32)
        side[...] = rf3[...].reshape(ROWS, HD).T
        pseudo = opb[...] - side[mine, :] * (1.0 / 16)
        moment = MOMENTUM_DECAY * omb[...] + pseudo
        new = opb[...] - factor * (pseudo + MOMENTUM_DECAY * moment)
        oob[...] = new
        omnb[...] = moment
        side[...] = jnp.zeros_like(side)
        side[mine, :] = new
        tf4[...] = side[...].T.astype(BF16).reshape(4, FR, HD)
        local(oob, oo_hbm)
        local(omnb, omn_hbm)
        for n, (i, to) in enumerate(zip(xs, xdev)):
            send(tf4.at[i], rf4.at[n], to, "d", "d")

    def outer_4():
        landed(rf4, "d")
        rf5[zh] = add(tf4[x], rf4[0], rf4[1], rf4[2]).astype(BF16)
        for to in zdev:
            send(rf5.at[zh], rf5.at[zh], to, "e", "e")

    def outer_5():
        landed(rf5.at[pl.ds(0, 3)], "e")
        for to in xdev:
            send(rf5, rf6.at[x], to, "f", "f")
        rf6[x] = rf5[...]

    def outer_6():
        landed(rf6.at[pl.ds(0, 3)], "f")
        for i in range(4):
            for j in range(4):
                rows, cols = slice(i * FR, (i + 1) * FR), slice(j * HD, (j + 1) * HD)
                blend = LOCAL_SHARE * fr[rows, cols].astype(F32)
                blend = blend + (1.0 - LOCAL_SHARE) * rf6[i, j].astype(F32)
                fout[rows, cols] = blend.astype(BF16)
        local(fout, of_hbm.at[0])

    for i, step in enumerate((outer_0, outer_1, outer_2, outer_3, outer_4, outer_5, outer_6)):
        todo[200 + i] = step
    for copy in w_local:
        copy.wait()
    landed(wg.at[0, 0, z, y], "ws")
    for number in ORDER:
        todo[number]()
    two_heads = ow_hbm.at[0, :, pl.ds(0, 2 * HD)]
    landed(two_heads, "w")
    for copy in locals_started[11:]:
        copy.wait()
    for sent in ("A0", "B0", "A1", "B1"):
        left(xb.at[0, pl.ds(0, 14 * SHARE * HD // D), :], sent)
    left(wg.at[0, 0, z, y], "ws")
    left(two_heads, "w")
    left(cb.at[0], "c")
    for s in range(STEPS):
        left(xb.at[s, pl.ds(TOK, TOK), :], "x" + str(s))
    for sent, ref in (("a", rf1), ("b", rf2), ("g", rf3.at[pl.ds(0, 3)]), ("d", rf4),
                      ("e", rf5.at[pl.ds(0, 3)]), ("f", rf6.at[pl.ds(0, 3)])):
        left(ref, sent)


def shards(
    layer_input, cotangent, key_weight, key_gain, fragment, outer_params, outer_momentum, plan
):
    tokens = layer_input.shape[2] * lax.axis_size("fsdp")
    inner_rate = 0.5 * math.sqrt(D / tokens)
    any_spec = pl.BlockSpec(memory_space=pl.ANY)
    vmem = lambda *shape, dtype=BF16: pltpu.VMEM(shape, dtype)
    hc, zr = HD // 2, SHARE - CUT
    results = pl.pallas_call(
        functools.partial(kernel, inner_rate),
        out_shape=(
            jax.ShapeDtypeStruct(key_weight.shape, BF16),
            jax.ShapeDtypeStruct(fragment.shape, BF16),
            jax.ShapeDtypeStruct(outer_params.shape[::-1], F32),
            jax.ShapeDtypeStruct(outer_momentum.shape[::-1], F32),
        ),
        in_specs=[any_spec] * 8,
        out_specs=[any_spec] * 4,
        scratch_shapes=[
            vmem(STEPS, 2 * TOK, D),
            vmem(STEPS, 2 * TOK, 2 * HD),
            vmem(STEPS, 2, NZ, NY, SHARE, HD),
            vmem(2, 2 * TOK, HD, dtype=F32),
            vmem(2, HD, 2 * TOK),
            vmem(STEPS, 2, NZ, NY, HD, CUT),
            vmem(STEPS, 2, NZ, NY, HD, zr),
            vmem(STEPS, 2, 2, NZ, hc, CUT),
            vmem(STEPS, 2, 2, NZ, HD, CUT),
            vmem(STEPS, 2, HD, CUT),
            vmem(STEPS, 2, HD, CUT),
            vmem(STEPS, 2, NY, HD, zr),
            vmem(STEPS, 2, 2, hc, zr),
            vmem(STEPS, 2, 2, HD, zr),
            vmem(2, SHARE, HD),
            vmem(ROWS, 4 * HD),
            vmem(32, ROWS, dtype=F32),
            vmem(32, ROWS, dtype=F32),
            vmem(3, FR, 4 * HD),
            vmem(4, FR, HD),
            vmem(3, FR, HD),
            vmem(4, FR, HD, dtype=F32),
            vmem(4, FR, HD),
            vmem(3, FR, HD),
            vmem(4, FR, HD),
            vmem(4, 4, FR, HD),
            vmem(ROWS, 4 * HD),
            vmem(32, ROWS, dtype=F32),
            vmem(32, ROWS, dtype=F32),
            vmem(HD, ROWS, dtype=F32),
            vmem(4, HD, dtype=F32),
            pltpu.SMEM((1,), jnp.int32),
            pltpu.SemaphoreType.REGULAR,
            pltpu.SemaphoreType.DMA((SENT,)),
            pltpu.SemaphoreType.DMA((CAME,)),
            pltpu.SemaphoreType.DMA((16,)),
        ],
        compiler_params=pltpu.CompilerParams(
            collective_id=0, has_side_effects=True, vmem_limit_bytes=56 << 20
        ),
        cost_estimate=pl.CostEstimate(
            flops=4 * 2 * 256 * D * 512, bytes_accessed=8 << 20, transcendentals=0
        ),
    )(
        layer_input,
        cotangent,
        key_weight,
        key_gain.reshape(4, HD),
        fragment,
        outer_params.T,
        outer_momentum.T,
        plan,
    )
    new_weight, new_fragment, new_outer, new_moment = pl.pallas_call(
        hand_over,
        out_shape=[jax.ShapeDtypeStruct(a.shape, a.dtype) for a in results],
        in_specs=[any_spec] * 4,
        out_specs=[any_spec] * 4,
        scratch_shapes=[pltpu.VMEM(a.shape, a.dtype) for a in results]
        + [pltpu.SemaphoreType.DMA((4,))] * 2,
    )(*results)
    return new_weight, new_fragment, new_outer.T, new_moment.T


def hand_over(*refs):
    n = (len(refs) - 2) // 3
    came, gone = refs[-2:]
    loads = [pltpu.make_async_copy(refs[i], refs[2 * n + i], came.at[i]) for i in range(n)]
    stores = [pltpu.make_async_copy(refs[2 * n + i], refs[n + i], gone.at[i]) for i in range(n)]
    for copy in loads:
        copy.start()
    for load, store in zip(loads, stores):
        load.wait()
        store.start()
    for copy in stores:
        copy.wait()


def solution(mesh):
    placed = (
        P("rep", None, "fsdp", None),
        P("rep", None, "fsdp", None),
        P("rep", "fsdp", None),
        P(),
        P("rep", "fsdp", None),
        P("fsdp", "rep"),
        P("fsdp", "rep"),
        P(),
    )
    return jax.shard_map(
        shards,
        mesh=mesh,
        in_specs=placed,
        out_specs=(
            P("rep", "fsdp", None),
            P("rep", "fsdp", None),
            P("fsdp", "rep"),
            P("fsdp", "rep"),
        ),
        check_vma=False,
    )
```

time: 323 us -> 88.2 us (0.27)
  waiting for transfers between devices: 214 us -> 0 us
  Pallas kernels: 0 us -> 86.6 us
  blocking collectives: 37.9 us -> 0 us
  local copies, waits for them, and re-layouts: 24.4 us -> 0 us
  matrix products: 21.2 us -> 0 us
  between operations: 16.2 us -> 1.45 us
  other arithmetic: 5.72 us -> 0 us
    unnamed x8 -> x0, waiting for transfers between devices: 124 us -> none
    all_gather x2 -> x0, waiting for transfers between devices: 90.1 us -> none  [project_keys(): lax.all_gather(weight_rows, 'fsdp', axis=0, tiled=True)]
    pallas_call x0 -> x2, Pallas kernels: none -> 86.6 us  [the longest x1 84.7 us: shards(): pl.pallas_call(functools.partial(kernel, inner_rate), out_shape=(jax.Shap...]
    all_gather x1 -> x0, blocking collectives: 37.9 us -> none  [shards(): lax.all_gather(new_outer.astype(jnp.bfloat16), 'rep', axis=1, tiled=True)]
    unnamed x19 -> x0, local copies, waits for them, and re-layouts: 21.3 us -> none
    dot_general x4 -> x0, matrix products: 21.2 us -> none  [the longest x2 11.6 us: grad_rows(): lax.dot_general(inputs, key_slope, (((0,), (0,)), ((), ())), preferred_el...]
  transfers between devices with their start and end apart: 5 -> 0, of which waited for: 5 -> 0; matrix products, arithmetic and copies ran while one was open for 8% -> 0% of each run, Pallas kernels for 0% -> 0%
where the time goes in v2:
time: 88.2 us; the launch traced here: 88.1 us
  Pallas kernels  86.6 us (98%)
  between operations  1.45 us (2%)
    pallas_call x1, Pallas kernels, shards(): pl.pallas_call(functools.partial(kernel, inner_rate), out_shape=(jax.Shap...  84.7 us
    pallas_call x1, Pallas kernels, shards(): pl.pallas_call(hand_over, out_shape=[jax.ShapeDtypeStruct(a.shape, a.dtyp...  1.89 us

profile of v2, /device:TPU:1, one launch (start us, length us, event | category | flops | bytes accessed | tf_op | source)
XLA Modules:
  0.0 88.1 jit_solution(4585131747684247589)
XLA Ops:
  1.3 84.7 %shard_map.111 = (bf16[1,320,512]{2,1,0:T(8,128)(2,1)}, bf16[1,320,512]{2,1,0:T(8,128)(2,1)}, f32[32,320]{1,0:T(8,128)}, f32[32,320]{1,0:T(8,128)}) custom-call(bf16[1,2,256,5120]{3,2,1,0:T(8,128)(2,1)} %x_hbm.1, bf16[1,2,256,512]{3,2,1,0:T(8,128)(2,1)} %c_hbm.1, bf16[1,320,512]{2,1,0:T(8,128)(2,1)} %w_hbm.1, f32[4,128]{1,0:T(4,128)} %bitcast.9, ...), custom_call_target="tpu_custom_call" | custom-call | flops 5368709120 | bytes 8388608 | tf_op jit(solution)/shard_map/pallas_call | solution.py:512
  86.0 1.9 %shard_map.112 = (bf16[1,320,512]{2,1,0:T(8,128)(2,1)}, bf16[1,320,512]{2,1,0:T(8,128)(2,1)}, f32[32,320]{1,0:T(8,128)}, f32[32,320]{1,0:T(8,128)}) custom-call(bf16[1,320,512]{2,1,0:T(8,128)(2,1)} %get-tuple-element.12.refs_0_, bf16[1,320,512]{2,1,0:T(8,128)(2,1)} %get-tuple-element.13.refs_1_, f32[32,320]{1,0:T(8,128)} %get-tuple-element.14.refs_2_, ...), custom_call_target="tpu_custom_call" | custom-call | tf_op jit(solution)/shard_map/pallas_call | solution.py:576

commit v3 on v2

--- a/solution.py
+++ b/solution.py
@@ -17,13 +17,13 @@
 LOCAL_SHARE = 0.25
 
 ORDER = (
-    51, 1, 2, 0, 50, 200, 52, 4, 3, 5, 55, 7, 54, 201, 9, 6, 53, 11, 57, 12,
-    10, 8, 62, 61, 56, 63, 13, 14, 60, 59, 58, 15, 16, 17, 64, 18, 65, 66, 20, 22,
-    68, 21, 69, 19, 67, 24, 202, 26, 23, 25, 74, 70, 27, 72, 71, 73, 28, 101, 102, 75,
-    76, 29, 100, 203, 77, 104, 103, 78, 151, 105, 107, 106, 112, 79, 150, 108, 109, 111, 110, 152,
-    204, 153, 154, 113, 114, 155, 157, 156, 162, 115, 116, 158, 159, 163, 160, 161, 118, 117, 164, 122,
-    121, 165, 166, 120, 119, 167, 168, 205, 170, 172, 171, 127, 124, 169, 174, 123, 125, 126, 173, 177,
-    176, 175, 206, 128, 129, 130, 178, 179, 180,
+    1, 200, 0, 50, 3, 4, 5, 6, 7, 2, 51, 52, 9, 12, 201, 8, 10, 11, 55, 13,
+    56, 57, 14, 53, 54, 62, 15, 16, 60, 17, 61, 58, 59, 63, 18, 64, 20, 22, 21, 19,
+    65, 66, 68, 23, 25, 27, 67, 24, 202, 26, 71, 70, 72, 29, 100, 28, 74, 101, 69, 76,
+    73, 77, 75, 102, 105, 203, 103, 107, 104, 106, 78, 151, 112, 79, 150, 111, 108, 113, 109, 152,
+    110, 114, 154, 204, 153, 155, 156, 157, 162, 115, 116, 163, 158, 160, 161, 159, 117, 118, 164, 121,
+    122, 165, 166, 168, 167, 119, 205, 170, 171, 172, 127, 120, 174, 169, 176, 124, 123, 173, 175, 177,
+    125, 126, 129, 206, 178, 128, 130, 179, 180,
 )
 
 MESH = pl.DeviceIdType.MESH

time: 88.2 us -> 85.9 us (0.974)
  Pallas kernels: 86.6 us -> 84.3 us
    pallas_call x1, Pallas kernels: 84.7 us -> 82.4 us  [shards(): pl.pallas_call(functools.partial(kernel, inner_rate), out_shape=(jax.Shap...]
where the time goes in v3:
time: 85.9 us; the launch traced here: 85.8 us
  Pallas kernels  84.3 us (98%)
  between operations  1.45 us (2%)
    pallas_call x1, Pallas kernels, shards(): pl.pallas_call(functools.partial(kernel, inner_rate), out_shape=(jax.Shap...  82.4 us
    pallas_call x1, Pallas kernels, shards(): pl.pallas_call(hand_over, out_shape=[jax.ShapeDtypeStruct(a.shape, a.dtyp...  1.89 us

profile of v3, /device:TPU:1, one launch (start us, length us, event | category | flops | bytes accessed | tf_op | source)
XLA Modules:
  0.0 85.8 jit_solution(15094296193169920282)
XLA Ops:
  1.3 82.4 %shard_map.111 = (bf16[1,320,512]{2,1,0:T(8,128)(2,1)}, bf16[1,320,512]{2,1,0:T(8,128)(2,1)}, f32[32,320]{1,0:T(8,128)}, f32[32,320]{1,0:T(8,128)}) custom-call(bf16[1,2,256,5120]{3,2,1,0:T(8,128)(2,1)} %x_hbm.1, bf16[1,2,256,512]{3,2,1,0:T(8,128)(2,1)} %c_hbm.1, bf16[1,320,512]{2,1,0:T(8,128)(2,1)} %w_hbm.1, f32[4,128]{1,0:T(4,128)} %bitcast.9, ...), custom_call_target="tpu_custom_call" | custom-call | flops 5368709120 | bytes 8388608 | tf_op jit(solution)/shard_map/pallas_call | solution.py:512
  83.7 1.9 %shard_map.112 = (bf16[1,320,512]{2,1,0:T(8,128)(2,1)}, bf16[1,320,512]{2,1,0:T(8,128)(2,1)}, f32[32,320]{1,0:T(8,128)}, f32[32,320]{1,0:T(8,128)}) custom-call(bf16[1,320,512]{2,1,0:T(8,128)(2,1)} %get-tuple-element.12.refs_0_, bf16[1,320,512]{2,1,0:T(8,128)(2,1)} %get-tuple-element.13.refs_1_, f32[32,320]{1,0:T(8,128)} %get-tuple-element.14.refs_2_, ...), custom_call_target="tpu_custom_call" | custom-call | tf_op jit(solution)/shard_map/pallas_call | solution.py:576

commit v4 on v3

--- a/solution.py
+++ b/solution.py
@@ -17,13 +17,13 @@
 LOCAL_SHARE = 0.25
 
 ORDER = (
-    1, 200, 0, 50, 3, 4, 5, 6, 7, 2, 51, 52, 9, 12, 201, 8, 10, 11, 55, 13,
-    56, 57, 14, 53, 54, 62, 15, 16, 60, 17, 61, 58, 59, 63, 18, 64, 20, 22, 21, 19,
-    65, 66, 68, 23, 25, 27, 67, 24, 202, 26, 71, 70, 72, 29, 100, 28, 74, 101, 69, 76,
-    73, 77, 75, 102, 105, 203, 103, 107, 104, 106, 78, 151, 112, 79, 150, 111, 108, 113, 109, 152,
-    110, 114, 154, 204, 153, 155, 156, 157, 162, 115, 116, 163, 158, 160, 161, 159, 117, 118, 164, 121,
-    122, 165, 166, 168, 167, 119, 205, 170, 171, 172, 127, 120, 174, 169, 176, 124, 123, 173, 175, 177,
-    125, 126, 129, 206, 178, 128, 130, 179, 180,
+    1, 0, 2, 51, 3, 4, 5, 50, 200, 7, 6, 9, 8, 12, 13, 10, 11, 53, 54, 55,
+    52, 56, 57, 62, 14, 15, 16, 31, 201, 58, 60, 59, 61, 17, 18, 63, 64, 20, 21, 22,
+    65, 66, 81, 19, 24, 23, 25, 67, 26, 27, 70, 68, 71, 72, 28, 73, 69, 101, 202, 29,
+    100, 74, 75, 102, 76, 77, 103, 104, 105, 203, 106, 107, 78, 151, 79, 150, 112, 109, 111, 110,
+    108, 152, 113, 114, 204, 153, 154, 155, 156, 157, 162, 115, 116, 131, 163, 159, 160, 158, 161, 117,
+    118, 164, 121, 122, 165, 166, 181, 167, 168, 120, 119, 205, 171, 172, 170, 127, 174, 124, 173, 123,
+    125, 169, 126, 177, 175, 176, 206, 128, 129, 178, 130, 179, 180,
 )
 
 MESH = pl.DeviceIdType.MESH
@@ -147,8 +147,8 @@
 
     barrier = pltpu.get_barrier_semaphore()
     plane = [(rep, z * 8 + yp * 2), (rep, z * 8 + ym * 2), (rep, zo * 8 + y * 2)]
-    plane += [(zh * 4 + i, z * 8 + y * 2) for i in xs]
     depth = [(i * 4 + x, z * 8 + y * 2 + 1) for i in zs]
+    depth += [(zh * 4 + i, z * 8 + y * 2 + 1) for i in xs]
     for to in plane + depth:
         pl.semaphore_signal(barrier, inc=1, device_id=to, device_id_type=MESH)
 
@@ -195,7 +195,7 @@
 
     todo = {}
     lo, hi = pl.ds(0, HD // 2), pl.ds(HD // 2, HD // 2)
-    groups = dict(puu="k3", pdd="k3", qdz="k3", quz="k4", quuz="k4", qddz="k4", pzuu="k4", pzdd="k4",
+    groups = dict(puu="k3", pdd="k3", qdz="k3", quz="k3", quuz="k4", qddz="k4", pzuu="k4", pzdd="k4",
                   Pu1="rp", Pu2="rp", Pd1="rp", Pd2="rp", z0="uq", Qu1="uq", Qu2="uq", Qd1="uq", Qd2="uq")
 
     def inner(s, h):
@@ -289,17 +289,17 @@
             acc[...] += project((z, ym), (zo, y))
 
         def k3():
-            take("k3", w.at[z, y])
-            acc[...] += project((z, y2), (zo, yp))
+            take("k3", cb.at[0, pl.ds(0, (2 * SHARE - TOP) // 2), :])
+            acc[...] += project((z, y2), (zo, yp), (zo, ym))
 
         def k4():
-            take("k4", cb.at[0, pl.ds(0, (2 * SHARE - TOP) // 2), :])
+            take("k4", w.at[z, y])
             if h == 0 and s == 0:
                 c_local[0].wait()
                 c_local[1].wait()
                 landed(cb.at[0], "c")
                 gain_local.wait()
-            kv = (acc[...] + project((zo, ym), (zo, y2))) * D**-0.5
+            kv = (acc[...] + project((zo, y2))) * D**-0.5
             inverse = lax.rsqrt(jnp.mean(kv * kv, axis=-1, keepdims=True) + 1e-06)
             u = kv * inverse
             gain = gain_ref[pl.ds(2 * c + h, 1), :]
@@ -307,21 +307,25 @@
             slope = (pulled - u * jnp.mean(pulled * u, axis=-1, keepdims=True)) * inverse
             sl[...] = slope.T.astype(BF16)
 
+        def one(bz, by):
+            at = pl.multiple_of((bz * NY + by) * SHARE, HD)
+            part = jnp.dot(sl[...], xb[s, :, pl.ds(at, SHARE)], preferred_element_type=F32)
+            mp[bz, by] = part[:, :CUT].astype(BF16)
+            mq[bz, by] = part[:, CUT:].astype(BF16)
+
         def grad(by):
-            lhs = sl[...]
-
-            def one(bz, carry):
-                at = pl.multiple_of((bz * NY + by) * SHARE, HD)
-                part = jnp.dot(lhs, xb[s, :, pl.ds(at, SHARE)], preferred_element_type=F32)
-                mp[bz, by] = part[:, :CUT].astype(BF16)
-                mq[bz, by] = part[:, CUT:].astype(BF16)
+            def step(bz, carry):
+                one(bz, by)
                 return carry
 
-            lax.fori_loop(0, NZ, one, 0)
+            lax.fori_loop(0, NZ, step, 0)
 
         def g2():
-            grad(y2)
+            one(zo, y2)
             put("z2", mq.at[zo, y2], q1.at[y2], across)
+
+        def g2b():
+            one(z, y2)
             put("Pu", mp.at[:, y2, lo], p1.at[0], up)
             put("Pd", mp.at[:, y2, hi], p1.at[1], down)
 
@@ -403,7 +407,7 @@
             gp=g_p, gq=g_q, gz=g_z, a_qu=a_qu, a_qd=a_qd, a_pz=a_pz, a_pu=a_pu, a_pd=a_pd,
             a_quu=a_quu, a_qdd=a_qdd, a_pzu=a_pzu, a_pzd=a_pzd, k1=k1, k2=k2, k3=k3, k4=k4,
             g2=g2, gu=gu, gd=gd, g0=g0, r_z2=r_z2, r_pu=r_pu, r_pd=r_pd, r_zp=r_zp, r_zm=r_zm,
-            r_qu=r_qu, r_qd=r_qd, r_p=r_p, uq=uq, up=up_, w=write,
+            r_qu=r_qu, r_qd=r_qd, r_p=r_p, uq=uq, up=up_, w=write, g2b=g2b,
         )
         for i, step in enumerate(steps.values()):
             todo[100 * s + 50 * h + i] = step
@@ -413,6 +417,7 @@
             inner(s, h)
 
     def outer_0():
+        meet_depth()
         for n, (i, to) in enumerate(zip(xs, xdev)):
             src = f_hbm.at[0, pl.ds(pl.multiple_of(i * FR, 16), FR), :]
             send(src, rf1.at[n], to, "a", "a")
@@ -424,7 +429,6 @@
         total = add(mine, rf1[0], rf1[1], rf1[2]).astype(BF16)
         for i in range(4):
             tf2[i] = total[:, i * HD : (i + 1) * HD]
-        meet_depth()
         for n, (i, to) in enumerate(zip(zs, zdev)):
             send(tf2.at[i], rf2.at[n], to, "b", "b")
 

time: 85.9 us -> 83.6 us (0.973)
  Pallas kernels: 84.3 us -> 82 us
    pallas_call x1, Pallas kernels: 82.4 us -> 80.1 us  [shards(): pl.pallas_call(functools.partial(kernel, inner_rate), out_shape=(jax.Shap...]
where the time goes in v4:
time: 83.6 us; the launch traced here: 83.5 us
  Pallas kernels  82 us (98%)
  between operations  1.45 us (2%)
    pallas_call x1, Pallas kernels, shards(): pl.pallas_call(functools.partial(kernel, inner_rate), out_shape=(jax.Shap...  80.1 us
    pallas_call x1, Pallas kernels, shards(): pl.pallas_call(hand_over, out_shape=[jax.ShapeDtypeStruct(a.shape, a.dtyp...  1.89 us

profile of v4, /device:TPU:1, one launch (start us, length us, event | category | flops | bytes accessed | tf_op | source)
XLA Modules:
  0.0 83.5 jit_solution(14578773286143759461)
XLA Ops:
  1.3 80.1 %shard_map.111 = (bf16[1,320,512]{2,1,0:T(8,128)(2,1)}, bf16[1,320,512]{2,1,0:T(8,128)(2,1)}, f32[32,320]{1,0:T(8,128)}, f32[32,320]{1,0:T(8,128)}) custom-call(bf16[1,2,256,5120]{3,2,1,0:T(8,128)(2,1)} %x_hbm.1, bf16[1,2,256,512]{3,2,1,0:T(8,128)(2,1)} %c_hbm.1, bf16[1,320,512]{2,1,0:T(8,128)(2,1)} %w_hbm.1, f32[4,128]{1,0:T(4,128)} %bitcast.9, ...), custom_call_target="tpu_custom_call" | custom-call | flops 5368709120 | bytes 8388608 | tf_op jit(solution)/shard_map/pallas_call | solution.py:516
  81.4 1.9 %shard_map.112 = (bf16[1,320,512]{2,1,0:T(8,128)(2,1)}, bf16[1,320,512]{2,1,0:T(8,128)(2,1)}, f32[32,320]{1,0:T(8,128)}, f32[32,320]{1,0:T(8,128)}) custom-call(bf16[1,320,512]{2,1,0:T(8,128)(2,1)} %get-tuple-element.12.refs_0_, bf16[1,320,512]{2,1,0:T(8,128)(2,1)} %get-tuple-element.13.refs_1_, f32[32,320]{1,0:T(8,128)} %get-tuple-element.14.refs_2_, ...), custom_call_target="tpu_custom_call" | custom-call | tf_op jit(solution)/shard_map/pallas_call | solution.py:580

commit v5 on v4

--- a/solution.py
+++ b/solution.py
@@ -583,7 +583,7 @@
         in_specs=[any_spec] * 4,
         out_specs=[any_spec] * 4,
         scratch_shapes=[pltpu.VMEM(a.shape, a.dtype) for a in results]
-        + [pltpu.SemaphoreType.DMA((4,))] * 2,
+        + [pltpu.SemaphoreType.DMA((6,))] * 2,
     )(*results)
     return new_weight, new_fragment, new_outer.T, new_moment.T
 
@@ -591,8 +591,22 @@
 def hand_over(*refs):
     n = (len(refs) - 2) // 3
     came, gone = refs[-2:]
-    loads = [pltpu.make_async_copy(refs[i], refs[2 * n + i], came.at[i]) for i in range(n)]
-    stores = [pltpu.make_async_copy(refs[2 * n + i], refs[n + i], gone.at[i]) for i in range(n)]
+    parts = []
+    for i in range(n):
+        if len(refs[i].shape) == 3:
+            size = refs[i].shape[1] // 2
+            parts += [(i, (0, pl.ds(j * size, size))) for j in range(2)]
+        else:
+            parts.append((i, (slice(None),)))
+    pick = lambda i, at: refs[i].at[at]
+    loads = [
+        pltpu.make_async_copy(pick(i, at), pick(2 * n + i, at), came.at[j])
+        for j, (i, at) in enumerate(parts)
+    ]
+    stores = [
+        pltpu.make_async_copy(pick(2 * n + i, at), pick(n + i, at), gone.at[j])
+        for j, (i, at) in enumerate(parts)
+    ]
     for copy in loads:
         copy.start()
     for load, store in zip(loads, stores):

time: 83.6 us -> 83.6 us (level)
  no operation moved by 1% of the time
where the time goes in v5:
time: 83.6 us; the launch traced here: 83.5 us
  Pallas kernels  82.1 us (98%)
  between operations  1.45 us (2%)
    pallas_call x1, Pallas kernels, shards(): pl.pallas_call(functools.partial(kernel, inner_rate), out_shape=(jax.Shap...  80.1 us
    pallas_call x1, Pallas kernels, shards(): pl.pallas_call(hand_over, out_shape=[jax.ShapeDtypeStruct(a.shape, a.dtyp...  1.95 us

profile of v5, /device:TPU:1, one launch (start us, length us, event | category | flops | bytes accessed | tf_op | source)
XLA Modules:
  0.0 83.5 jit_solution(1293135736780505028)
XLA Ops:
  1.3 80.1 %shard_map.111 = (bf16[1,320,512]{2,1,0:T(8,128)(2,1)}, bf16[1,320,512]{2,1,0:T(8,128)(2,1)}, f32[32,320]{1,0:T(8,128)}, f32[32,320]{1,0:T(8,128)}) custom-call(bf16[1,2,256,5120]{3,2,1,0:T(8,128)(2,1)} %x_hbm.1, bf16[1,2,256,512]{3,2,1,0:T(8,128)(2,1)} %c_hbm.1, bf16[1,320,512]{2,1,0:T(8,128)(2,1)} %w_hbm.1, f32[4,128]{1,0:T(4,128)} %bitcast.9, ...), custom_call_target="tpu_custom_call" | custom-call | flops 5368709120 | bytes 8388608 | tf_op jit(solution)/shard_map/pallas_call | solution.py:516
  81.4 1.9 %shard_map.112 = (bf16[1,320,512]{2,1,0:T(8,128)(2,1)}, bf16[1,320,512]{2,1,0:T(8,128)(2,1)}, f32[32,320]{1,0:T(8,128)}, f32[32,320]{1,0:T(8,128)}) custom-call(bf16[1,320,512]{2,1,0:T(8,128)(2,1)} %get-tuple-element.12.refs_0_, bf16[1,320,512]{2,1,0:T(8,128)(2,1)} %get-tuple-element.13.refs_1_, f32[32,320]{1,0:T(8,128)} %get-tuple-element.14.refs_2_, ...), custom_call_target="tpu_custom_call" | custom-call | tf_op jit(solution)/shard_map/pallas_call | solution.py:580
